TPU v7x, 256 devices: a whole 4x4x8 slice. The times are simulated.
256 devices in a mesh: dp: 8 (over z), expert: 32 (over x, y, core).
Axes of the slice: x: 4, y: 4, z: 8, core: 2. Of those that a mesh axis runs over, the one named last changes fastest.
Arguments:
- tokens: bfloat16 [8192, 7168], P('expert', 'dp'), may hold values from -6 to 6
- out_grad: bfloat16 [8192, 7168], P('expert', 'dp'), may hold values from -6 to 6
- routes: int32 [8192, 2], P('expert'), may hold values from 0 to 31, all different within a row; in each aligned block of 256 rows (0 to 255, 256 to 511, ...) at most 32 rows name the same one
- route_weights: float32 [8192, 2], P('expert'), may hold values from 0.2 to 1
- w_gate: bfloat16 [32, 7168, 1024], P('expert', 'dp'), may hold values from -0.0625 to 0.0625
- w_up: bfloat16 [32, 7168, 1024], P('expert', 'dp'), may hold values from -0.0625 to 0.0625
- w_down: bfloat16 [32, 1024, 7168], P('expert', None, 'dp'), may hold values from -0.1875 to 0.1875
- p_in: bfloat16 [32, 2, 16, 7168], P('expert', None, None, 'dp'), may hold values from -0.0625 to 0.0625
- q_in: bfloat16 [32, 2, 16, 1024], P('expert'), may hold values from -0.75 to 0.75
- p_down: bfloat16 [32, 16, 1024], P('expert'), may hold values from -0.75 to 0.75
- q_down: bfloat16 [32, 16, 7168], P('expert', None, 'dp'), may hold values from -0.0625 to 0.0625
- lam: float32 [32, 3, 16], P('expert'), may hold values from 0.2 to 1
- rank_mask: int32 [32, 3, 16], P('expert'), may hold values 0 or 1
Outputs:
- input_grad: bfloat16 [8192, 7168], P('expert', 'dp')
- grad_q_in: float32 [32, 2, 16, 1024], P('expert', None, None, 'dp')
- grad_p_in: float32 [32, 2, 16, 7168], P('expert', None, None, 'dp')
- grad_p_down: float32 [32, 16, 1024], P('expert', None, 'dp')
- grad_q_down: float32 [32, 16, 7168], P('expert', None, 'dp')
- grad_lam: float32 [32, 3, 16], P('expert')
Inputs may be any that keep to these rules, and one draw needn't show every extreme that they name: `routes`: each row names 2 different experts. In each aligned block of 256 rows no expert is named more than 32 times, a bound that some block reaches.
All inputs are finite; a program needn't handle non-finite values. No bound on the sum of `rank_mask` on one device may be relied on, other than what follows from the above.
Results may differ from a plain program's by a relative error of at most 0.03.
Values may be sent and summed in bfloat16 or wider, within the bound.
A program may use at most 128 MiB of HBM per device.

v0:
```python
import functools

import jax
import jax.numpy as jnp
from jax import lax
from jax.experimental import pallas as pl
from jax.experimental.pallas import tpu as pltpu
from jax.sharding import PartitionSpec as P

MESH = pl.DeviceIdType.MESH
F32 = jnp.float32
BF16 = jnp.bfloat16
HIGH = lax.Precision.HIGHEST

D_BLOCK = 896
FF = 1024
RANK = 16
TOK = 256
CAP = 32
N_DP = 8
N_EXPERT = 32
CHUNKS = 4
SHARES = 8
ROWS = SHARES * CAP
WIDTHS = (FF, FF, FF + 128)
CUTS = (512, 512, 640)
PIECES = (512, 512, 512, 640)
WA = 2 * FF + 128
OFFSETS = (
    ((0, 0), (1, 0), (3, 0), (0, 1)),
    ((1, 1), (3, 3), (3, 1), (1, 3)),
    ((2, 1), (2, 3), (0, 2), (2, 2)),
    ((1, 2), (3, 2), (0, 3), (2, 0)),
)


def dot_nn(a, b, precision=None):
    return lax.dot_general(a, b, (((1,), (0,)), ((), ())), precision=precision, preferred_element_type=F32)


def dot_nt(a, b, precision=None):
    return lax.dot_general(a, b, (((1,), (1,)), ((), ())), precision=precision, preferred_element_type=F32)


def dot_tn(a, b):
    return lax.dot_general(a, b, (((0,), (0,)), ((), ())), preferred_element_type=F32)


def pick(values, chunk):
    if isinstance(chunk, int):
        return values[chunk]
    out = values[0]
    for k in range(1, len(values)):
        out = jnp.where(chunk == k, values[k], out)
    return out


def kernel(
    routes_ref,
    weights_ref,
    tokens_hbm,
    grads_hbm,
    wg_hbm,
    wu_hbm,
    wd_hbm,
    p_in_ref,
    q_in_ref,
    p_down_ref,
    q_down_ref,
    lam_ref,
    mask_ref,
    in_grad_ref,
    gq_ref,
    gp_ref,
    gpd_ref,
    gqd_ref,
    gl_ref,
    tok,
    out_grad,
    wg,
    wu,
    wd,
    p_tok,
    p_grad,
    q_all,
    hot,
    send_t,
    send_g,
    recv_t,
    recv_g,
    part_gate,
    part_up,
    part_down,
    ring_gate,
    ring_up,
    ring_down,
    gathered,
    near,
    route_out,
    returned,
    hidden_own,
    acc_in,
    acc_pd,
    acc_lam,
    scale_row,
    pos,
    fin_send,
    fin_recv,
    load_sem,
    t_send,
    t_recv,
    g_send,
    g_recv,
    r_send,
    r_recv,
    rs_send,
    rs_recv,
    ag_send,
    ag_recv,
    fin_ssem,
    fin_rsem,
):
    z = lax.axis_index("dp")
    e = lax.axis_index("expert")
    ex = e // 8
    ey = (e // 2) % 4
    ec = e % 2
    right = (z + 1) % N_DP
    left = (z + N_DP - 1) % N_DP

    def expert_at(chunk, j, sign):
        dx = pick([o[j // 2][0] for o in OFFSETS], chunk)
        dy = pick([o[j // 2][1] for o in OFFSETS], chunk)
        x = (ex + 4 + sign * dx) % 4
        y = (ey + 4 + sign * dy) % 4
        return (x * 4 + y) * 2 + (ec + j) % 2

    loads = []
    for k, (src, dst) in enumerate(
        (
            (tokens_hbm, tok),
            (grads_hbm, out_grad),
            (wg_hbm.at[0], wg),
            (wu_hbm.at[0], wu),
            (wd_hbm.at[0], wd),
        )
    ):
        copy = pltpu.make_async_copy(src, dst, load_sem.at[k])
        copy.start()
        loads.append(copy)

    barrier = pltpu.get_barrier_semaphore()
    for k in range(1, N_EXPERT):
        pl.semaphore_signal(barrier, inc=1, device_id=(z, (e + k) % N_EXPERT), device_id_type=MESH)
    for k in range(1, N_DP):
        pl.semaphore_signal(barrier, inc=1, device_id=((z + k) % N_DP, e), device_id_type=MESH)

    expert_iota = lax.broadcasted_iota(jnp.int32, (N_EXPERT, TOK), 0)
    named0 = (expert_iota == routes_ref[0:1, :]).astype(F32)
    named1 = (expert_iota == routes_ref[1:2, :]).astype(F32)
    earlier = (
        lax.broadcasted_iota(jnp.int32, (TOK, TOK), 0) < lax.broadcasted_iota(jnp.int32, (TOK, TOK), 1)
    ).astype(BF16)
    before = dot_nn((named0 + named1).astype(BF16), earlier)
    pos[0:1, :] = jnp.sum(named0 * before, axis=0, keepdims=True) + CAP * routes_ref[0:1, :].astype(F32)
    pos[1:2, :] = jnp.sum(named1 * before, axis=0, keepdims=True) + CAP * routes_ref[1:2, :].astype(F32)

    def t_copy(chunk, j):
        return pltpu.make_async_remote_copy(
            send_t.at[chunk, j], recv_t.at[chunk, j], t_send.at[chunk], t_recv.at[chunk],
            device_id=(z, expert_at(chunk, j, -1)), device_id_type=MESH,
        )

    def g_copy(chunk, j):
        return pltpu.make_async_remote_copy(
            send_g.at[chunk, j], recv_g.at[chunk, j], g_send.at[chunk], g_recv.at[chunk],
            device_id=(z, expert_at(chunk, j, -1)), device_id_type=MESH,
        )

    def r_copy(chunk, j):
        return pltpu.make_async_remote_copy(
            route_out.at[chunk, j], returned.at[chunk, j], r_send.at[chunk], r_recv.at[chunk],
            device_id=(z, expert_at(chunk, j, 1)), device_id_type=MESH,
        )

    def send_all(chunk, copy_of, src, dst, sem):
        for j in range(SHARES):
            if j == 0:
                @pl.when(chunk > 0)
                def _():
                    copy_of(chunk, 0).start()

                @pl.when(chunk == 0)
                def _():
                    pltpu.make_async_copy(src.at[chunk, 0], dst.at[chunk, 0], sem.at[chunk]).start()
            else:
                copy_of(chunk, j).start()

    def wait_chunk(ref, sem, chunk):
        pltpu.make_async_copy(ref.at[chunk], ref.at[chunk], sem.at[chunk]).wait()

    slot_iota = lax.broadcasted_iota(jnp.int32, (CAP, TOK), 0)

    def route_chunk(chunk):
        pos0, pos1 = pos[0:1, :], pos[1:2, :]
        weight0, weight1 = weights_ref[0:1, :], weights_ref[1:2, :]
        slot_weights = []
        for j in range(SHARES):
            target = (slot_iota + CAP * expert_at(chunk, j, -1)).astype(F32)
            hit0, hit1 = target == pos0, target == pos1
            hot[chunk, j * CAP:(j + 1) * CAP, :] = jnp.where(hit0 | hit1, 1.0, 0.0).astype(BF16)
            weight = jnp.where(hit0, weight0, 0.0) + jnp.where(hit1, weight1, 0.0)
            slot_weights.append(jnp.sum(weight, axis=1, keepdims=True))
        picked = dot_nn(hot[chunk], tok[...])
        send_t[chunk] = picked.astype(BF16).reshape(SHARES, CAP, D_BLOCK)
        picked = dot_nn(hot[chunk], out_grad[...])
        for j in range(SHARES):
            send_g[chunk, j] = (slot_weights[j] * picked[j * CAP:(j + 1) * CAP, :]).astype(BF16)

    def route_send(chunk):
        send_all(chunk, t_copy, send_t, recv_t, t_recv)
        send_all(chunk, g_copy, send_g, recv_g, g_recv)

    def project(chunk, source, weights, part, transposed=False):
        @pl.loop(0, 2)
        def _(n):
            x = source[chunk].reshape(ROWS, D_BLOCK)
            at = pl.ds(pl.multiple_of(n * 512, 512), 512)
            out = dot_nt(x, weights[at, :]) if transposed else dot_nn(x, weights[:, at])
            part[chunk, :, :, at] = out.astype(BF16).reshape(SHARES, CAP, 512)

    def forward_gate(chunk):
        wait_chunk(recv_t, t_recv, chunk)
        project(chunk, recv_t, wg, part_gate)

    def forward_up(chunk):
        project(chunk, recv_t, wu, part_up)

    def forward_down(chunk):
        wait_chunk(recv_g, g_recv, chunk)
        ranks = dot_nt(recv_t[chunk].reshape(ROWS, D_BLOCK), p_tok[...])
        ranks = ranks + dot_nt(recv_g[chunk].reshape(ROWS, D_BLOCK), p_grad[...])
        part_down[chunk, :, :, pl.ds(FF, 128)] = ranks.astype(BF16).reshape(SHARES, CAP, 128)
        project(chunk, recv_g, wd, part_down, True)

    rings = ((part_gate, ring_gate), (part_up, ring_up), (part_down, ring_down))

    def ring_copy(stream, chunk, way, step):
        part, ring = rings[stream]
        width, cut = WIDTHS[stream], CUTS[stream]
        if step == 0:
            cols = pl.ds(0, cut) if way == 0 else pl.ds(cut, width - cut)
            src = part.at[chunk, (z + 4) % N_DP, :, cols]
            dst = ring.at[chunk, way, 0, :, cols]
        else:
            src, dst = ring.at[chunk, way, step - 1], ring.at[chunk, way, step]
        return pltpu.make_async_remote_copy(
            src, dst, rs_send.at[stream, way, step], rs_recv.at[stream, way, step],
            device_id=(right if way == 0 else left, e), device_id_type=MESH,
        )

    def start_next(copy, chunk):
        if not (isinstance(chunk, int) and chunk == 0):
            @pl.when(chunk > 0)
            def _():
                copy.wait_send()

        copy.start()

    def ring_start(stream, chunk):
        for way in range(2):
            start_next(ring_copy(stream, chunk, way, 0), chunk)

    def ring_step(stream, chunk, step):
        part, ring = rings[stream]
        width, cut = WIDTHS[stream], CUTS[stream]
        for way in range(2):
            ring_copy(stream, chunk, way, step - 1).wait_recv()
            target = (z + 4 - step) % N_DP if way == 0 else (z + 4 + step) % N_DP
            if step == 1:
                lo, hi = (0, cut) if way == 0 else (cut, width)
                total = ring[chunk, way, 0, :, lo:hi].astype(F32) + part[chunk, target, :, lo:hi].astype(F32)
                ring[chunk, way, 0, :, lo:hi] = total.astype(BF16)
                lo, hi = (cut, width) if way == 0 else (0, cut)
                ring[chunk, way, 0, :, lo:hi] = part[chunk, target, :, lo:hi]
            else:
                total = ring[chunk, way, step - 1].astype(F32) + part[chunk, target].astype(F32)
                ring[chunk, way, step - 1] = total.astype(BF16)
            start_next(ring_copy(stream, chunk, way, step), chunk)

    def ring_end(chunk):
        for stream in range(3):
            for way in range(2):
                ring_copy(stream, chunk, way, 3).wait_recv()

    def gather_copy(half, chunk, way, step, arriving=False):
        hops = step + 1 if arriving else step
        owner = (z + N_DP - hops) % N_DP if way == 0 else (z + hops) % N_DP
        ref = gathered.at[chunk, owner, :, pl.ds(half * 512, PIECES[half])]
        return pltpu.make_async_remote_copy(
            ref, ref, ag_send.at[half, way, step], ag_recv.at[half, way, step],
            device_id=(right if way == 0 else left, e), device_id_type=MESH,
        )

    def gather_ways(half, step):
        return (half // 2,) if step == 3 else (0, 1)

    def gather_start(chunk, pieces):
        for half in pieces:
            for way in range(2):
                start_next(gather_copy(half, chunk, way, 0), chunk)

    def gather_step(half, chunk, step):
        for way in range(2):
            gather_copy(half, chunk, way, step - 1, True).wait_recv()
            if way in gather_ways(half, step):
                start_next(gather_copy(half, chunk, way, step), chunk)

    def gather_end(chunk):
        for half in range(4):
            gather_copy(half, chunk, half // 2, 3, True).wait_recv()

    def hidden_chunk(chunk):
        at = pl.ds(FF, 128)
        ranks = (
            part_down[chunk, z, :, at].astype(F32)
            + ring_down[chunk, 0, 3, :, at].astype(F32)
            + ring_down[chunk, 1, 3, :, at].astype(F32)
        )
        scaled = ranks * scale_row[0:1, :]
        high = scaled.astype(BF16)
        low = (scaled - high.astype(F32)).astype(BF16)
        both = jnp.concatenate([high, low], axis=0)

        def tile(n, back):
            at = pl.ds(pl.multiple_of(n * 256, 256), 256)
            at_up = pl.ds(pl.multiple_of(n * 256 + FF, 256), 256)
            at_down = pl.ds(pl.multiple_of(n * 256 + 2 * FF, 256), 256)

            def low_rank(cols):
                extra = dot_nn(both, q_all[:, cols])
                return extra[:CAP] + extra[CAP:]

            def summed(part, ring, cols):
                return (
                    part[chunk, z, :, cols].astype(F32)
                    + ring[chunk, 0, 3, :, cols].astype(F32)
                    + ring[chunk, 1, 3, :, cols].astype(F32)
                )

            gate_pre = summed(part_gate, ring_gate, at) + low_rank(at)
            up_pre = summed(part_up, ring_up, at) + low_rank(at_up)
            hidden_grad = summed(part_down, ring_down, at) + low_rank(at_down)
            sigmoid = 1.0 / (1.0 + jnp.exp(-gate_pre))
            activated = gate_pre * sigmoid
            slope = sigmoid * (1.0 + gate_pre * (1.0 - sigmoid))
            hidden = (activated * up_pre).astype(BF16)
            gate_grad = (hidden_grad * up_pre * slope).astype(BF16)
            up_grad = (hidden_grad * activated).astype(BF16)
            hidden_own[:, at] = hidden
            place = n * 256 + 512 * (n // 2)
            gathered[chunk, z, :, pl.ds(pl.multiple_of(place, 256), 256)] = gate_grad
            gathered[chunk, z, :, pl.ds(pl.multiple_of(place + 512, 256), 256)] = up_grad
            back = back + dot_nt(gate_grad, q_all[:, at])
            back = back + dot_nt(up_grad, q_all[:, at_up])
            return back + dot_nt(hidden, q_all[:, at_down])

        back = lax.fori_loop(0, 2, tile, jnp.zeros((CAP, 128), F32))
        gather_start(chunk, (0, 1))
        back = lax.fori_loop(2, 4, tile, back)
        lane = lax.broadcasted_iota(jnp.int32, (CAP, 128), 1)
        side = jnp.where(lane < 64, back * scale_row[0:1, :], scaled).astype(BF16)
        gathered[chunk, z, :, pl.ds(2 * FF, 128)] = side
        gather_start(chunk, (2, 3))
        acc_lam[...] += jnp.sum(ranks * back, axis=0, keepdims=True)
        acc_pd[...] += dot_tn(side, hidden_own[...])[96:112]

    def back_rows(rows, n):
        def cols(lo, width):
            return rows[:, :, pl.ds(lo, width)].reshape(n * CAP, width)

        total = dot_nt(cols(0, 512), wg[:, :512]) + dot_nt(cols(512, 512), wu[:, :512])
        total = total + dot_nt(cols(1024, 512), wg[:, 512:]) + dot_nt(cols(1536, 512), wu[:, 512:])
        total = total + dot_nn(cols(2 * FF, 128)[:, :64], p_tok[:64])
        return total.astype(BF16).reshape(n, CAP, D_BLOCK)

    def back_chunk(chunk):
        route_out[chunk] = back_rows(gathered.at[chunk], SHARES)
        send_all(chunk, r_copy, route_out, returned, r_recv)

    opposite = (z + 4) % N_DP

    def back_near(chunk):
        for k in range(SHARES - 1):
            near[k] = gathered[chunk, (z + 5 + k) % N_DP]
        total = back_rows(near, SHARES - 1)
        for k in range(SHARES - 1):
            route_out[chunk, (z + 5 + k) % N_DP] = total[k]
        for j in range(SHARES):
            @pl.when(opposite != j)
            def _():
                r_copy(chunk, j).start()

    def back_far(chunk):
        total = back_rows(gathered.at[chunk, pl.ds(opposite, 1)], 1)
        route_out[chunk, opposite] = total[0]
        for j in range(SHARES):
            @pl.when(opposite == j)
            def _():
                r_copy(chunk, j).start()

    def small_chunk(chunk):
        side = gathered[chunk, :, :, pl.ds(2 * FF, 128)].reshape(ROWS, 128)
        grad_p = dot_tn(side, recv_t[chunk].reshape(ROWS, D_BLOCK))
        gp_ref[0, 0] += grad_p[0:16]
        gp_ref[0, 1] += grad_p[16:32]
        gqd_ref[0] += dot_tn(side, recv_g[chunk].reshape(ROWS, D_BLOCK))[32:48]
        mine = pl.multiple_of(z * 128 + 512 * (z // 4), 128)
        gate_mine = gathered[chunk, :, :, pl.ds(mine, 128)].reshape(ROWS, 128)
        up_mine = gathered[chunk, :, :, pl.ds(pl.multiple_of(mine + 512, 128), 128)].reshape(ROWS, 128)
        gq_ref[0, 0] += dot_tn(side, gate_mine)[64:80]
        gq_ref[0, 1] += dot_tn(side, up_mine)[80:96]

    def combine_chunk(chunk):
        wait_chunk(returned, r_recv, chunk)
        acc_in[...] += dot_tn(hot[chunk], returned[chunk].reshape(ROWS, D_BLOCK))

    loads[0].wait()
    loads[1].wait()

    route_chunk(0)
    pl.semaphore_wait(barrier, N_EXPERT - 1 + N_DP - 1)
    route_send(0)

    @pl.loop(1, CHUNKS)
    def _(chunk):
        route_chunk(chunk)

    p_tok[...] = jnp.zeros_like(p_tok)
    p_grad[...] = jnp.zeros_like(p_grad)
    for base in (0, 64):
        p_tok[base:base + 16, :] = p_in_ref[0, 0]
        p_tok[base + 16:base + 32, :] = p_in_ref[0, 1]
        p_grad[base + 32:base + 48, :] = q_down_ref[0]

    q_all[...] = jnp.zeros_like(q_all)
    q_all[0:16, 0:FF] = q_in_ref[0, 0]
    q_all[16:32, FF:2 * FF] = q_in_ref[0, 1]
    q_all[32:48, 2 * FF:] = p_down_ref[0]
    spread = (
        lax.broadcasted_iota(jnp.int32, (RANK, 128), 0) == lax.broadcasted_iota(jnp.int32, (RANK, 128), 1) % 16
    ).astype(F32)
    lanes = lax.broadcasted_iota(jnp.int32, (1, 128), 1)
    wide = jnp.zeros((1, 128), F32)
    for k in range(3):
        scale = lam_ref[k] * mask_ref[k].astype(F32)
        wide = wide + jnp.where((lanes % 64) // 16 == k, dot_nn(scale, spread, HIGH), 0.0)
    scale_row[...] = wide
    acc_in[...] = jnp.zeros_like(acc_in)
    acc_pd[...] = jnp.zeros_like(acc_pd)
    acc_lam[...] = jnp.zeros_like(acc_lam)
    gq_ref[...] = jnp.zeros_like(gq_ref)
    gp_ref[...] = jnp.zeros_like(gp_ref)
    gqd_ref[...] = jnp.zeros_like(gqd_ref)
    loads[2].wait()
    loads[3].wait()
    loads[4].wait()

    def fin_copy(k):
        peer = (z + k) % N_DP
        return pltpu.make_async_remote_copy(
            fin_send.at[peer], fin_recv.at[k], fin_ssem.at[k], fin_rsem.at[k],
            device_id=(peer, e), device_id_type=MESH,
        )

    wait_chunk(recv_t, t_recv, 0)
    project(0, recv_t, wg, part_gate)
    ring_start(0, 0)
    route_send(1)
    forward_up(0)
    ring_start(1, 0)
    forward_down(0)
    ring_start(2, 0)

    @pl.loop(0, CHUNKS + 1)
    def _(i):
        ringing = i < CHUNKS
        gathering = i > 0
        more = i < CHUNKS - 1
        for step in range(1, 4):
            @pl.when(ringing)
            def _():
                for stream in range(3):
                    ring_step(stream, i, step)

            @pl.when(gathering)
            def _():
                for piece in range(4):
                    gather_step(piece, i - 1, step)

            if step == 1:
                @pl.when(i == CHUNKS)
                def _():
                    for k in range(N_DP):
                        fin_send[k, 0:16, :] = acc_pd[:, k * 128:(k + 1) * 128]
                        fin_send[k, 16:24, :] = jnp.broadcast_to(acc_lam[...], (8, 128))
                    for k in range(1, N_DP):
                        fin_copy(k).start()

                @pl.when(i > 1)
                def _():
                    back_chunk(i - 2)
                    small_chunk(i - 2)

            if step == 2:
                @pl.when(more)
                def _():
                    forward_gate(i + 1)
                    forward_up(i + 1)

                @pl.when(i > 2)
                def _():
                    combine_chunk(i - 3)

            if step == 3:
                @pl.when(i == CHUNKS)
                def _():
                    back_near(CHUNKS - 1)

                @pl.when(more)
                def _():
                    ring_start(0, i + 1)
                    ring_start(1, i + 1)
                    forward_down(i + 1)
                    ring_start(2, i + 1)

                @pl.when(i < CHUNKS - 2)
                def _():
                    route_send(i + 2)

        @pl.when(ringing)
        def _():
            ring_end(i)
            hidden_chunk(i)

        @pl.when(gathering)
        def _():
            gather_end(i - 1)

    back_far(CHUNKS - 1)
    small_chunk(CHUNKS - 1)
    combine_chunk(CHUNKS - 2)
    for k in range(1, N_DP):
        fin_copy(k).wait_recv()
    fin_recv[0] = fin_send[z]
    total = fin_recv[z]
    for k in range(1, N_DP):
        total = total + fin_recv[(z + N_DP - k) % N_DP]
    gpd_ref[0] = total[0:16]
    for k in range(3):
        lam_total = jnp.where(lanes // 16 == k, total[16:17], 0.0)
        gl_ref[k] = dot_nt(lam_total, spread, HIGH) * mask_ref[k].astype(F32)
    combine_chunk(CHUNKS - 1)
    in_grad_ref[...] = acc_in[...].astype(BF16)

    for k in range(1, N_DP):
        fin_copy(k).wait_send()

    @pl.loop(0, CHUNKS)
    def _(chunk):
        for ref, sem in ((send_t, t_send), (send_g, g_send), (route_out, r_send)):
            @pl.when(chunk > 0)
            def _():
                pltpu.make_async_copy(ref.at[chunk], ref.at[chunk], sem.at[chunk]).wait()

            @pl.when(chunk == 0)
            def _():
                sent = ref.at[chunk, pl.ds(1, SHARES - 1)]
                pltpu.make_async_copy(sent, sent, sem.at[chunk]).wait()

    for step in range(4):
        for way in range(2):
            for stream in range(3):
                ring_copy(stream, CHUNKS - 1, way, step).wait_send()
            for half in range(4):
                if way in gather_ways(half, step):
                    gather_copy(half, CHUNKS - 1, way, step).wait_send()


def deliver(*refs):
    for k in range(6):
        refs[k + 6][...] = refs[k][...]


def body(
    tokens, out_grad, routes, route_weights, w_gate, w_up, w_down, p_in, q_in, p_down, q_down, lam, rank_mask
):
    vmem = pl.BlockSpec(memory_space=pltpu.VMEM)
    hbm = pl.BlockSpec(memory_space=pl.ANY)
    dma = pltpu.SemaphoreType.DMA
    grid_rows = (CHUNKS, SHARES, CAP)
    scratch = [
        pltpu.VMEM((TOK, D_BLOCK), BF16),
        pltpu.VMEM((TOK, D_BLOCK), BF16),
        pltpu.VMEM((D_BLOCK, FF), BF16),
        pltpu.VMEM((D_BLOCK, FF), BF16),
        pltpu.VMEM((FF, D_BLOCK), BF16),
        pltpu.VMEM((128, D_BLOCK), BF16),
        pltpu.VMEM((128, D_BLOCK), BF16),
        pltpu.VMEM((128, 3 * FF), BF16),
        pltpu.VMEM((CHUNKS, ROWS, TOK), BF16),
        pltpu.VMEM(grid_rows + (D_BLOCK,), BF16),
        pltpu.VMEM(grid_rows + (D_BLOCK,), BF16),
        pltpu.VMEM(grid_rows + (D_BLOCK,), BF16),
        pltpu.VMEM(grid_rows + (D_BLOCK,), BF16),
        *[pltpu.VMEM(grid_rows + (width,), BF16) for width in WIDTHS],
        *[pltpu.VMEM((CHUNKS, 2, 4, CAP, width), BF16) for width in WIDTHS],
        pltpu.VMEM(grid_rows + (WA,), BF16),
        pltpu.VMEM((SHARES - 1, CAP, WA), BF16),
        pltpu.VMEM(grid_rows + (D_BLOCK,), BF16),
        pltpu.VMEM(grid_rows + (D_BLOCK,), BF16),
        pltpu.VMEM((CAP, FF), BF16),
        pltpu.VMEM((TOK, D_BLOCK), F32),
        pltpu.VMEM((RANK, FF), F32),
        pltpu.VMEM((1, 128), F32),
        pltpu.VMEM((1, 128), F32),
        pltpu.VMEM((2, TOK), F32),
        pltpu.VMEM((N_DP, 24, 128), F32),
        pltpu.VMEM((N_DP, 24, 128), F32),
        dma((5,)),
        dma((CHUNKS,)),
        dma((CHUNKS,)),
        dma((CHUNKS,)),
        dma((CHUNKS,)),
        dma((CHUNKS,)),
        dma((CHUNKS,)),
        dma((3, 2, 4)),
        dma((3, 2, 4)),
        dma((4, 2, 4)),
        dma((4, 2, 4)),
        dma((N_DP,)),
        dma((N_DP,)),
    ]
    results = pl.pallas_call(
        kernel,
        out_shape=(
            jax.ShapeDtypeStruct((TOK, D_BLOCK), BF16),
            jax.ShapeDtypeStruct((1, 2, RANK, FF // N_DP), F32),
            jax.ShapeDtypeStruct((1, 2, RANK, D_BLOCK), F32),
            jax.ShapeDtypeStruct((1, RANK, FF // N_DP), F32),
            jax.ShapeDtypeStruct((1, RANK, D_BLOCK), F32),
            jax.ShapeDtypeStruct((3, 1, RANK), F32),
        ),
        in_specs=[vmem, vmem, hbm, hbm, hbm, hbm, hbm, vmem, vmem, vmem, vmem, vmem, vmem],
        out_specs=(vmem,) * 6,
        scratch_shapes=scratch,
        compiler_params=pltpu.CompilerParams(
            collective_id=0, has_side_effects=True, vmem_limit_bytes=58 * 1024 * 1024
        ),
        name="adapter_backward",
    )(
        routes.T, route_weights.T, tokens, out_grad, w_gate, w_up, w_down, p_in, q_in, p_down, q_down,
        lam.transpose(1, 0, 2), rank_mask.transpose(1, 0, 2),
    )
    results = pl.pallas_call(
        deliver,
        out_shape=tuple(jax.ShapeDtypeStruct(r.shape, r.dtype) for r in results),
        in_specs=[vmem] * 6,
        out_specs=(vmem,) * 6,
        name="deliver",
    )(*results)
    return (*results[:5], results[5].transpose(1, 0, 2))


def solution(mesh):
    in_specs = (
        P("expert", "dp"),
        P("expert", "dp"),
        P("expert", None),
        P("expert", None),
        P("expert", "dp", None),
        P("expert", "dp", None),
        P("expert", None, "dp"),
        P("expert", None, None, "dp"),
        P("expert", None, None, None),
        P("expert", None, None),
        P("expert", None, "dp"),
        P("expert", None, None),
        P("expert", None, None),
    )
    out_specs = (
        P("expert", "dp"),
        P("expert", None, None, "dp"),
        P("expert", None, None, "dp"),
        P("expert", None, "dp"),
        P("expert", None, "dp"),
        P("expert", None, None),
    )
    return jax.shard_map(body, mesh=mesh, in_specs=in_specs, out_specs=out_specs, check_vma=False)
```

profile of v0, /device:TPU:1, one launch (start us, length us, event | category | flops | bytes accessed | tf_op | source)
XLA Modules:
  0.0 140.6 jit_solution(9276336516092480537)
XLA Ops:
  0.6 138.1 %adapter_backward.1 = (bf16[256,896]{1,0:T(8,128)(2,1)}, f32[1,2,16,128]{3,2,1,0:T(8,128)}, f32[1,2,16,896]{3,2,1,0:T(8,128)}, f32[1,16,128]{2,1,0:T(8,128)}, f3...) custom-call(s32[2,256]{1,0:T(2,128)} %bitcast.5, f32[2,256]{1,0:T(2,128)} %bitcast.6, bf16[256,896]{1,0:T(8,128)(2,1)} %tokens_hbm.1, ...), custom_call_target="tpu_custom_call" | custom-call | tf_op jit(solution)/shard_map/adapter_backward/pallas_call | solution.py:644
  138.7 1.9 %deliver.1 = (bf16[256,896]{1,0:T(8,128)(2,1)}, f32[1,2,16,128]{3,2,1,0:T(8,128)}, f32[1,2,16,896]{3,2,1,0:T(8,128)}, f32[1,16,128]{2,1,0:T(8,128)}, f32[1,16,896]{2,1,0:T(8,128)}, /*index=5*/f32[3,1,16]{2,1,0:T(1,128)}) custom-call(bf16[256,896]{1,0:T(8,128)(2,1)} %get-tuple-element.18.refs_0_, f32[1,2,16,128]{3,2,1,0:T(8,128)} %get-tuple-element.19.refs_1_, ...), custom_call_target="tpu_custom_call" | custom-call | tf_op jit(solution)/shard_map/deliver/pallas_call | solution.py:665
where the time goes:
time: 141 us
  Pallas kernels  140 us (99%)
    pallas_call x1, Pallas kernels, body(): pl.pallas_call(kernel, out_shape=(jax.ShapeDtypeStruct((TOK, D_BLOCK), BF...  138 us

commit v1 on v0

--- a/solution.py
+++ b/solution.py
@@ -499,6 +499,22 @@
                     gather_step(piece, i - 1, step)
 
             if step == 1:
+                @pl.when(i > 1)
+                def _():
+                    back_chunk(i - 2)
+                    small_chunk(i - 2)
+
+            if step == 2:
+                @pl.when(more)
+                def _():
+                    forward_gate(i + 1)
+                    forward_up(i + 1)
+
+                @pl.when(i > 2)
+                def _():
+                    combine_chunk(i - 3)
+
+            if step == 3:
                 @pl.when(i == CHUNKS)
                 def _():
                     for k in range(N_DP):
@@ -507,22 +523,6 @@
                     for k in range(1, N_DP):
                         fin_copy(k).start()
 
-                @pl.when(i > 1)
-                def _():
-                    back_chunk(i - 2)
-                    small_chunk(i - 2)
-
-            if step == 2:
-                @pl.when(more)
-                def _():
-                    forward_gate(i + 1)
-                    forward_up(i + 1)
-
-                @pl.when(i > 2)
-                def _():
-                    combine_chunk(i - 3)
-
-            if step == 3:
                 @pl.when(i == CHUNKS)
                 def _():
                     back_near(CHUNKS - 1)

time: 141 us -> 141 us (level)
  no operation moved by 1% of the time
where the time goes in v1:
time: 141 us
  Pallas kernels  141 us (100%)
    pallas_call x1, Pallas kernels, body(): pl.pallas_call(kernel, out_shape=(jax.ShapeDtypeStruct((TOK, D_BLOCK), BF...  139 us

profile of v1, /device:TPU:1, one launch (start us, length us, event | category | flops | bytes accessed | tf_op | source)
XLA Modules:
  0.0 141.3 jit_solution(9847105473084367135)
XLA Ops:
  0.6 138.7 %adapter_backward.1 = (bf16[256,896]{1,0:T(8,128)(2,1)}, f32[1,2,16,128]{3,2,1,0:T(8,128)}, f32[1,2,16,896]{3,2,1,0:T(8,128)}, f32[1,16,128]{2,1,0:T(8,128)}, f3...) custom-call(s32[2,256]{1,0:T(2,128)} %bitcast.5, f32[2,256]{1,0:T(2,128)} %bitcast.6, bf16[256,896]{1,0:T(8,128)(2,1)} %tokens_hbm.1, ...), custom_call_target="tpu_custom_call" | custom-call | tf_op jit(solution)/shard_map/adapter_backward/pallas_call | solution.py:644
  139.4 1.9 %deliver.1 = (bf16[256,896]{1,0:T(8,128)(2,1)}, f32[1,2,16,128]{3,2,1,0:T(8,128)}, f32[1,2,16,896]{3,2,1,0:T(8,128)}, f32[1,16,128]{2,1,0:T(8,128)}, f32[1,16,896]{2,1,0:T(8,128)}, /*index=5*/f32[3,1,16]{2,1,0:T(1,128)}) custom-call(bf16[256,896]{1,0:T(8,128)(2,1)} %get-tuple-element.18.refs_0_, f32[1,2,16,128]{3,2,1,0:T(8,128)} %get-tuple-element.19.refs_1_, ...), custom_call_target="tpu_custom_call" | custom-call | tf_op jit(solution)/shard_map/deliver/pallas_call | solution.py:665
